TPU v7x, 512 devices: a whole 4x8x8 slice. The times are simulated.
512 devices in a mesh: feat: 64 (over z, x, core), dom: 8 (over y).
Axes of the slice: x: 4, y: 8, z: 8, core: 2. Of those that a mesh axis runs over, the one named last changes fastest.
Arguments:
- features: bfloat16 [8, 1024, 8192], P('dom', 'feat'), may hold values from -6 to 6
- weight: bfloat16 [1024, 1024], P('feat'), may hold values from -0.1875 to 0.1875
- tile_bank: bfloat16 [4, 128, 128], replicated, may hold values from -0.5 to 0.5
- neighbors: int32 [8, 64, 8], P('dom'), may hold values from 0 to 95, as said below
- tile_ids: int32 [8, 64, 8], P('dom'), may hold values from 0 to 3
- edge_weight: bfloat16 [8, 64, 8], P('dom'), may hold values from 0.099609375 to 1
- counts: int32 [8, 64], P('dom'), may hold values from 2 to 8, as said below
- boundary: int32 [8, 8, 4], P(None, 'dom'), may hold values from 0 to 63
- cotangent: bfloat16 [8, 1024, 8192], P('dom', None, 'feat'), may hold values from -16 to 16
Outputs:
- activations: bfloat16 [8, 1024, 8192], P('dom', None, 'feat')
- feature_grad: bfloat16 [8, 1024, 8192], P('dom', 'feat')
- weight_grad: float32 [1024, 1024], P('feat')
Inputs may be any that keep to these rules, and one draw needn't show every extreme that they name: `neighbors`: slot 0 of block row r names r itself; slot 1 names an entry of 64 or more, and every entry from 64 to 95 is slot 1 of some row of each partition. `counts`: slots at or after a row's count are unused; each partition has a row with all 8 slots used.
All inputs are finite; a program needn't handle non-finite values.
Results may differ from a plain program's by a relative error of at most 0.015.
Values may be sent and summed in bfloat16 or wider, within the bound.
A program may use at most 64 MiB of HBM per device.

v0:
```python
import math

import jax
import jax.numpy as jnp
from jax import lax
from jax.sharding import PartitionSpec as P

TILE = 128
NBANK = 4
K = 8


def silu_slope(pre_act):
    sigmoid_v = jax.nn.sigmoid(pre_act)
    return sigmoid_v * (1.0 + pre_act * (1.0 - sigmoid_v))


def per_device(
    features, weight, tile_bank, neighbors, tile_ids, edge_weight, counts, boundary, cotangent
):
    columns = features[0]
    slices = columns.shape[0]
    vertices = columns.shape[1]
    block_count = vertices // TILE
    partitions = lax.axis_size("dom")
    per_pair = boundary.shape[2]
    blocks = columns.reshape(slices, block_count, TILE)
    wanted = boundary[:, 0, :].reshape(-1)
    outgoing = jnp.take(blocks, wanted, axis=1).reshape(slices, partitions, per_pair, TILE)
    link_ids = neighbors[0]
    selector = jnp.arange(NBANK, dtype=jnp.int32)
    slot_ids = jnp.arange(K, dtype=jnp.int32)
    active = (tile_ids[0][:, :, None] == selector[None, None, :]) & (
        slot_ids[None, :, None] < counts[0][:, None, None]
    )
    coeffs = jnp.where(active, edge_weight[0][:, :, None], jnp.zeros((), edge_weight.dtype))
    arrived = lax.all_to_all(outgoing, "dom", split_axis=1, concat_axis=1, tiled=True)
    far_blocks = arrived.reshape(slices, partitions * per_pair, TILE)
    pool_x = jnp.concatenate([blocks, far_blocks], axis=1)
    picked = jnp.take(pool_x, link_ids.reshape(-1), axis=1).reshape(slices, block_count, K, TILE)
    mixed_sum = jnp.einsum("rkt,frkv->rtfv", coeffs, picked, preferred_element_type=jnp.float32)
    mixed_bf = mixed_sum.astype(jnp.bfloat16)
    aggregated = (
        jnp.einsum("rtfv,tuv->fru", mixed_bf, tile_bank, preferred_element_type=jnp.float32)
        .astype(jnp.bfloat16)
        .reshape(slices, vertices)
    )
    row_view = lax.all_to_all(aggregated, "feat", split_axis=1, concat_axis=0, tiled=True)
    full_weight = lax.all_gather(weight, "feat", axis=0, tiled=True)
    pre_act = jnp.dot(full_weight, row_view, preferred_element_type=jnp.float32)
    activated = jax.nn.silu(pre_act).astype(jnp.bfloat16)
    slope_bf = (cotangent[0].astype(jnp.float32) * silu_slope(pre_act)).astype(jnp.bfloat16)
    feat_grad = lax.psum_scatter(
        lax.dot_general(
            slope_bf, row_view, (((1,), (1,)), ((), ())), preferred_element_type=jnp.float32
        ),
        "feat",
        scatter_dimension=0,
        tiled=True,
    )
    weight_sum = lax.psum(feat_grad.astype(jnp.bfloat16), "dom").astype(jnp.float32)
    vertex_total = partitions * vertices
    weight_grad = weight_sum * (1.0 / math.sqrt(vertex_total))
    agg_grad = lax.dot_general(
        full_weight, slope_bf, (((0,), (0,)), ((), ())), preferred_element_type=jnp.float32
    ).astype(jnp.bfloat16)
    grad_columns = lax.all_to_all(agg_grad, "feat", split_axis=0, concat_axis=1, tiled=True)
    back_mix = jnp.einsum(
        "fru,tuv->rtfv",
        grad_columns.reshape(slices, block_count, TILE),
        tile_bank,
        preferred_element_type=jnp.float32,
    ).astype(jnp.bfloat16)
    edge_grad = jnp.einsum("rkt,rtfv->rkfv", coeffs, back_mix, preferred_element_type=jnp.float32)
    pool_grad = jax.ops.segment_sum(
        edge_grad.reshape(block_count * K, slices, TILE),
        link_ids.reshape(-1),
        num_segments=block_count + partitions * per_pair,
    )
    sent_grad = (
        pool_grad[block_count:].reshape(partitions, per_pair, slices, TILE).astype(jnp.bfloat16)
    )
    landed_grad = lax.all_to_all(sent_grad, "dom", split_axis=0, concat_axis=0, tiled=True)
    own_grad = pool_grad[:block_count] + jax.ops.segment_sum(
        landed_grad.reshape(partitions * per_pair, slices, TILE).astype(jnp.float32),
        wanted,
        num_segments=block_count,
    )
    feature_grad = jnp.transpose(own_grad, (1, 0, 2)).reshape(slices, vertices).astype(jnp.bfloat16)
    return (activated[None], feature_grad[None], weight_grad)


def solution(mesh):
    in_specs = (
        P("dom", "feat", None),
        P("feat", None),
        P(),
        P("dom", None, None),
        P("dom", None, None),
        P("dom", None, None),
        P("dom", None),
        P(None, "dom", None),
        P("dom", None, "feat"),
    )
    out_specs = (P("dom", None, "feat"), P("dom", "feat", None), P("feat", None))
    return jax.shard_map(
        per_device, mesh=mesh, in_specs=in_specs, out_specs=out_specs, check_vma=False
    )
```

profile of v0, /device:TPU:6, one launch (start us, length us, event | category | flops | bytes accessed | tf_op | source)
XLA Modules:
  0.0 292.4 jit_solution(5098087952988998312)
XLA Ops:
  7.9 1.0 copy.53
  12.1 7.1 %all-to-all-start = ((bf16[16,8,4,128]{3,0,2,1:T(8,128)(2,1)}), bf16[16,8,4,128]{3,0,2,1:T(8,128)(2,1)S(1)}, u32[]{:S(2)}, u32[]{:S(2)}) async-start(bf16[16,8,4,128]{3,0,2,1:T(8,128)(2,1)} %broadcast_select_fusion), calls=%async_computation | async-start | bytes 262144 | tf_op jit(solution)/shard_map/all_to_all | solution.py:37
  23.2 5.1 %all-to-all-done = bf16[16,8,4,128]{3,0,2,1:T(8,128)(2,1)S(1)} async-done(((bf16[16,8,4,128]{3,0,2,1:T(8,128)(2,1)}), bf16[16,8,4,128]{3,0,2,1:T(8,128)(2,1)S(1)}, u32[]{:S(2)}, u32[]{:S(2)}) %all-to-all-start) | async-done | bytes 131104 | tf_op jit(solution)/shard_map/all_to_all | solution.py:37
  28.3 2.0 gather_fusion.1
  30.4 0.8 fusion.2
  31.2 1.1 fusion.6
  32.4 13.8 %all-to-all-start.1 = ((bf16[16,64,128]{2,0,1:T(8,128)(2,1)}), bf16[16,64,128]{2,0,1:T(8,128)(2,1)S(1)}, u32[]{:S(2)}, u32[]{:S(2)}) async-start(bf16[16,64,128]{2,0,1:T(8,128)(2,1)} %fusion.6), calls=%async_computation.1 | async-start | bytes 524288 | tf_op jit(solution)/shard_map/all_to_all | solution.py:48
  46.4 11.9 %all-to-all-done.1 = bf16[16,64,128]{2,0,1:T(8,128)(2,1)S(1)} async-done(((bf16[16,64,128]{2,0,1:T(8,128)(2,1)}), bf16[16,64,128]{2,0,1:T(8,128)(2,1)S(1)}, u32[]{:S(2)}, u32[]{:S(2)}) %all-to-all-start.1) | async-done | bytes 262176 | tf_op jit(solution)/shard_map/all_to_all | solution.py:48
  58.4 40.5 %all-gather.2.cloned.1.call-done = bf16[1024,1024]{1,0:T(8,128)(2,1)} async-done(((bf16[16,1024]{1,0:T(8,128)(2,1)}), bf16[1024,1024]{1,0:T(8,128)(2,1)}) %all-gather.2.cloned.1.call-update) | async-done | bytes 2097168 | tf_op jit(solution)/shard_map/all_gather | solution.py:49
  98.9 2.4 convolution_bitcast_fusion
  101.3 2.7 fusion.25
  104.0 1.6 copy-done.1
  106.2 0.8 copy.44
  107.0 7.6 %all-to-all-start.2 = ((bf16[64,16,128]{2,1,0:T(8,128)(2,1)}), bf16[64,16,128]{2,1,0:T(8,128)(2,1)S(1)}, u32[]{:S(2)}, u32[]{:S(2)}) async-start(bf16[64,16,128]{2,1,0:T(8,128)(2,1)} %bitcast.25), calls=%async_computation.2 | async-start | bytes 524288 | tf_op jit(solution)/shard_map/all_to_all | solution.py:67
  114.8 11.8 %all-to-all-done.2 = bf16[64,16,128]{2,1,0:T(8,128)(2,1)S(1)} async-done(((bf16[64,16,128]{2,1,0:T(8,128)(2,1)}), bf16[64,16,128]{2,1,0:T(8,128)(2,1)S(1)}, u32[]{:S(2)}, u32[]{:S(2)}) %all-to-all-start.2) | async-done | bytes 262176 | tf_op jit(solution)/shard_map/all_to_all | solution.py:67
  127.9 2.9 copy.46
  130.8 40.2 %scatter_fusion = f32[96,16,128]{2,1,0:T(8,128)S(1)} fusion(f32[96,16,128]{2,1,0:T(8,128)S(1)} %broadcast_in_dim.52, s32[512]{0:T(512)S(1)} %reshape.169, f32[512,16,128]{2,1,0:T(8,128)} %bitcast.83), kind=kCustom, calls=%fused_computation.2 | custom fusion | flops 1048576 | bytes 12584960 | tf_op jit(solution)/shard_map/scatter-add | solution.py:75
  171.7 6.7 %all-to-all-start.3 = ((bf16[8,4,16,128]{3,2,1,0:T(8,128)(2,1)}), bf16[8,4,16,128]{3,2,1,0:T(8,128)(2,1)S(1)}, u32[]{:S(2)}, u32[]{:S(2)}) async-start(bf16[8,4,16,128]{3,2,1,0:T(8,128)(2,1)} %bitcast.31), calls=%async_computation.3 | async-start | bytes 262144 | tf_op jit(solution)/shard_map/all_to_all | solution.py:83
  178.6 0.8 copy.49
  179.5 8.1 %all-to-all-done.3 = bf16[8,4,16,128]{3,2,1,0:T(8,128)(2,1)S(1)} async-done(((bf16[8,4,16,128]{3,2,1,0:T(8,128)(2,1)}), bf16[8,4,16,128]{3,2,1,0:T(8,128)(2,1)S(1)}, u32[]{:S(2)}, u32[]{:S(2)}) %all-to-all-start.3) | async-done | bytes 131104 | tf_op jit(solution)/shard_map/all_to_all | solution.py:83
  187.6 1.7 scatter_fusion.1
  190.2 64.2 %reduce-scatter.2.cloned.1.call-done = f32[16,1024]{1,0:T(8,128)} async-done(((f32[1024,1024]{1,0:T(8,128)}), f32[16,1024]{1,0:T(8,128)}) %reduce-scatter.2.cloned.1.call-update) | async-done | bytes 65552 | tf_op jit(solution)/shard_map/reduce_scatter | solution.py:53
  254.4 0.8 convert_element_type.82
  255.3 29.7 %psum.7 = bf16[16,1024]{1,0:T(8,128)(2,1)S(1)} all-reduce(bf16[16,1024]{1,0:T(8,128)(2,1)S(1)} %convert_element_type.82), channel_id=1, replica_groups=mesh['feat'=64,'dom'=8] {'dom'}, use_global_device_ids=true, to_apply=%region_3.4 | all-reduce | flops 16384 | bytes 65536 | tf_op jit(solution)/shard_map/psum | solution.py:61
  (51 shorter events, 12.6 us)
Async XLA Ops:
  7.2 24.1 %copy-start = (bf16[4,128,128]{2,1,0:T(8,128)(2,1)S(1)}, bf16[4,128,128]{2,1,0:T(8,128)(2,1)}, u32[]{:S(2)}) copy-start(bf16[4,128,128]{2,1,0:T(8,128)(2,1)} %param.11) | copy-start | bytes 393220
  7.2 91.7 %all-gather.2.cloned.1.call-start = ((), (), s32[]{:S(2)}) async-start(), calls=%async_computation.5 | async-start | bytes 2129920 | tf_op jit(solution)/shard_map/all_gather | solution.py:49
  12.1 16.2 %all-to-all-start = ((bf16[16,8,4,128]{3,0,2,1:T(8,128)(2,1)}), bf16[16,8,4,128]{3,0,2,1:T(8,128)(2,1)S(1)}, u32[]{:S(2)}, u32[]{:S(2)}) async-start(bf16[16,8,4,128]{3,0,2,1:T(8,128)(2,1)} %broadcast_select_fusion), calls=%async_computation | async-start | bytes 262144 | tf_op jit(solution)/shard_map/all_to_all | solution.py:37
  20.0 8.3 %copy-start.2 = (s32[1,64,8]{2,1,0:T(8,128)}, s32[1,64,8]{2,1,0:T(8,128)S(1)}, u32[]{:S(2)}) copy-start(s32[1,64,8]{2,1,0:T(8,128)S(1)} %copy.39) | copy-start | bytes 6148
  21.5 8.8 %copy-start.5 = (s32[64,8]{1,0:T(8,128)}, s32[64,8]{1,0:T(8,128)S(1)}, u32[]{:S(2)}) copy-start(s32[64,8]{1,0:T(8,128)S(1)} %copy.32) | copy-start | bytes 6148
  31.2 15.0 %copy-start.4 = (bf16[1,1024,128]{2,1,0:T(8,128)(2,1)S(1)}, bf16[1,1024,128]{2,1,0:T(8,128)(2,1)}, u32[]{:S(2)}) copy-start(bf16[1,1024,128]{2,1,0:T(8,128)(2,1)} %param.17) | copy-start | bytes 786436
  32.4 26.0 %all-to-all-start.1 = ((bf16[16,64,128]{2,0,1:T(8,128)(2,1)}), bf16[16,64,128]{2,0,1:T(8,128)(2,1)S(1)}, u32[]{:S(2)}, u32[]{:S(2)}) async-start(bf16[16,64,128]{2,0,1:T(8,128)(2,1)} %fusion.6), calls=%async_computation.1 | async-start | bytes 524288 | tf_op jit(solution)/shard_map/all_to_all | solution.py:48
  46.2 208.2 %reduce-scatter.2.cloned.1.call-start = ((), (), s32[]{:S(2)}) async-start(), calls=%async_computation.6 | async-start | bytes 4259840 | tf_op jit(solution)/shard_map/reduce_scatter | solution.py:53
  104.0 1.6 copy-start.1
  105.6 9.1 %copy-start.3 = (s32[1,64,8]{2,1,0:T(8,128)S(1)}, s32[1,64,8]{2,1,0:T(8,128)}, u32[]{:S(2)}) copy-start(s32[1,64,8]{2,1,0:T(8,128)} %copy-done.2) | copy-start | bytes 6148
  106.2 20.9 %copy-start.6 = (s32[64,8]{1,0:T(8,128)S(1)}, s32[64,8]{1,0:T(8,128)}, u32[]{:S(2)}) copy-start(s32[64,8]{1,0:T(8,128)} %copy-done.5) | copy-start | bytes 6148
  107.0 19.6 %all-to-all-start.2 = ((bf16[64,16,128]{2,1,0:T(8,128)(2,1)}), bf16[64,16,128]{2,1,0:T(8,128)(2,1)S(1)}, u32[]{:S(2)}, u32[]{:S(2)}) async-start(bf16[64,16,128]{2,1,0:T(8,128)(2,1)} %bitcast.25), calls=%async_computation.2 | async-start | bytes 524288 | tf_op jit(solution)/shard_map/all_to_all | solution.py:67
  171.7 15.8 %all-to-all-start.3 = ((bf16[8,4,16,128]{3,2,1,0:T(8,128)(2,1)}), bf16[8,4,16,128]{3,2,1,0:T(8,128)(2,1)S(1)}, u32[]{:S(2)}, u32[]{:S(2)}) async-start(bf16[8,4,16,128]{3,2,1,0:T(8,128)(2,1)} %bitcast.31), calls=%async_computation.3 | async-start | bytes 262144 | tf_op jit(solution)/shard_map/all_to_all | solution.py:83
Sparse Core Ops, SparseCore 0:
  11.4 87.4 all-gather.1
  104.2 150.2 reduce-scatter.1
where the time goes:
time: 294 us; the launch traced here: 292 us
  waiting for transfers between devices  142 us (48%)
  other arithmetic  46.6 us (16%)
  starting transfers between devices  35.4 us (12%)
  blocking collectives  29.7 us (10%)
  local copies, waits for them, and re-layouts  15.4 us (5%)
  between operations  14.3 us (5%)
  matrix products  8.89 us (3%)
    reduce_scatter x1, waiting for transfers between devices, per_device(): lax.psum_scatter(lax.dot_general(slope_bf, row_view, (((1,), (1,)), ((),...  64.2 us
    all_gather x1, waiting for transfers between devices, per_device(): full_weight = lax.all_gather(weight, 'feat', axis=0, tiled=True)  40.5 us
    scatter-add x1, other arithmetic, per_device(): jax.ops.segment_sum(edge_grad.reshape(block_count * K, slices, TILE), lin...  40.2 us
    psum x1, blocking collectives, per_device(): lax.psum(feat_grad.astype(jnp.bfloat16), 'dom').astype(jnp.float32)  29.7 us
    all_to_all x1, starting transfers between devices, per_device(): lax.all_to_all(aggregated, 'feat', split_axis=1, concat_axis=0, tiled=True)  13.8 us
    all_to_all x1, waiting for transfers between devices, per_device(): lax.all_to_all(aggregated, 'feat', split_axis=1, concat_axis=0, tiled=True)  11.9 us
    all_to_all x1, waiting for transfers between devices, per_device(): lax.all_to_all(agg_grad, 'feat', split_axis=0, concat_axis=1, tiled=True)  11.8 us
    all_to_all x1, waiting for transfers between devices, per_device(): lax.all_to_all(sent_grad, 'dom', split_axis=0, concat_axis=0, tiled=True)  8.05 us
  transfers between devices with their start and end apart: 6, of which 6 were waited for; matrix products, arithmetic and copies ran while one was open for 21% of the time, Pallas kernels for 0%

commit v1 on v0

v1 whole, which is shorter than its diff:
```python
import functools
import math

import jax
import jax.numpy as jnp
from jax import lax
from jax.experimental import pallas as pl
from jax.experimental.pallas import tpu as pltpu
from jax.sharding import PartitionSpec as P

TILE = 128
NBANK = 4
K = 8
ROWS = 16
GROUPS = 4
MESH = pl.DeviceIdType.MESH
F32 = jnp.float32
BF16 = jnp.bfloat16
SUB = 2

NT = (((1,), (1,)), ((), ()))


def dot(a, b):
    return jnp.dot(a, b, preferred_element_type=F32)


def kernel(
    nf,
    ny,
    per_pair,
    scale,
    bnd_ref,
    x_ref,
    w_ref,
    bank_ref,
    nbr_ref,
    tid_ref,
    ew_ref,
    cnt_ref,
    cot_ref,
    act_ref,
    fg_ref,
    wg_ref,
    shuf,
    xk,
    out_blocks,
    land,
    near,
    an_bf,
    af_bf,
    atn_bf,
    atf_bf,
    oht_bf,
    bank_u,
    mixed,
    send_a,
    view,
    view2,
    wbuf,
    slope,
    slope_t,
    slope2,
    send_g,
    cols,
    back,
    own,
    send_d,
    land_d,
    part,
    right_s,
    right_r,
    left_s,
    left_r,
    send_z,
    land_z,
    send_y,
    land_y,
    phase_s,
    phase_r,
    wring_s,
    wring_r,
    wpair_s,
    wpair_r,
    gring_s,
    gring_r,
):
    nb = nf
    chips = nf // 2
    chunk = nf * ROWS // ny
    per_chunk = chunk // ROWS
    half = chips * ROWS
    far = ny * ROWS
    lanes = NBANK * nb
    group = ROWS // GROUPS
    width = group * TILE
    right = ny // 2
    left = ny - 1 - right

    me = lax.axis_index("feat")
    dom = lax.axis_index("dom")
    core = lax.rem(me, 2)
    chip = lax.div(me, 2)
    partner = me + 1 - 2 * core

    def at_dom(step):
        return lax.rem(dom + step + ny, ny)

    def copy_to(src, dst, send_sem, recv_sem, feat_id, dom_id):
        return pltpu.make_async_remote_copy(
            src_ref=src,
            dst_ref=dst,
            send_sem=send_sem,
            recv_sem=recv_sem,
            device_id=(feat_id, dom_id),
            device_id_type=MESH,
        )

    def wait_bytes(ref, sem):
        pltpu.make_async_copy(ref, ref, sem).wait()

    barrier = pltpu.get_barrier_semaphore()

    def greet_dom(step, carry):
        pl.semaphore_signal(
            barrier, inc=1, device_id=(me, at_dom(step)), device_id_type=MESH
        )
        return carry

    def greet_feat(step, carry):
        pl.semaphore_signal(
            barrier, inc=1, device_id=(lax.rem(me + step, nf), dom), device_id_type=MESH
        )
        return carry

    lax.fori_loop(1, ny, greet_dom, 0)
    lax.fori_loop(1, nf, greet_feat, 0)

    for b in range(nb):
        shuf[b * ROWS : (b + 1) * ROWS, :] = x_ref[
            :, b * TILE : (b + 1) * TILE
        ].astype(F32)
    for f in range(ROWS):
        xk[f // group, :, (f % group) * TILE : (f % group + 1) * TILE] = shuf[
            pl.ds(f, nb, stride=ROWS), :
        ].astype(BF16)

    lane = lax.broadcasted_iota(jnp.int32, (1, far), 1)
    lane_q = lax.div(lane, ROWS)
    lane_g = lax.rem(lax.div(lane, per_pair), GROUPS)
    lane_j = lax.rem(lane, per_pair)
    wanted = jnp.full((1, far), -1, jnp.int32)
    for q in range(ny):
        for j in range(per_pair):
            wanted = jnp.where(
                (lane_q == q) & (lane_j == j), bnd_ref[j, q], wanted
            )
    row_b = lax.broadcasted_iota(jnp.int32, (nb, far), 0)
    hots = [
        jnp.where((row_b == wanted) & (lane_g == g), 1.0, 0.0) for g in range(GROUPS)
    ]
    for g in range(GROUPS):
        oht_bf[g] = hots[g].astype(BF16)
    hot = jnp.concatenate(hots, axis=0).T.astype(BF16)
    out_blocks[...] = (
        dot(hot, xk[...].reshape(GROUPS * nb, width))
        .astype(BF16)
        .reshape(ny, ROWS, width)
    )

    pl.semaphore_wait(barrier, nf + ny - 2)

    def send_blocks(step, carry):
        to = at_dom(step)
        copy_to(
            out_blocks.at[to], land.at[dom], phase_s.at[0], phase_r.at[0], me, to
        ).start()
        return carry

    lax.fori_loop(1, ny, send_blocks, 0)

    my_rows = pl.ds(pl.multiple_of(chip * ROWS, ROWS), ROWS)
    my_chunk = pl.ds(pl.multiple_of(dom * chunk, chunk), chunk)

    def send_weight(step, carry):
        to = lax.rem(me + 2 * step, nf)
        copy_to(
            w_ref.at[:, my_chunk],
            wbuf.at[dom, core, my_rows, :],
            phase_s.at[1],
            phase_r.at[1],
            to,
            dom,
        ).start()
        return carry

    lax.fori_loop(1, chips, send_weight, 0)
    wbuf[dom, core, my_rows, :] = w_ref[:, my_chunk]
    land[dom] = out_blocks[dom]

    for t in range(NBANK):
        bank_u[:, t * TILE : (t + 1) * TILE] = bank_ref[t]
    nbr = jnp.concatenate([nbr_ref[...]] * NBANK, axis=1)
    tid = jnp.concatenate([tid_ref[...]] * NBANK, axis=1)
    edge = jnp.concatenate([ew_ref[...].astype(F32)] * NBANK, axis=1)
    cnt = jnp.concatenate([cnt_ref[...]] * NBANK, axis=1)
    lane_t = lax.div(lax.broadcasted_iota(jnp.int32, (K, lanes), 1), nb)
    slot = lax.broadcasted_iota(jnp.int32, (K, lanes), 0)
    coeff = jnp.where((tid == lane_t) & (slot < cnt), edge, 0.0)
    near_c = lax.broadcasted_iota(jnp.int32, (nb, lanes), 0)
    far_l = lax.broadcasted_iota(jnp.int32, (far, lanes), 0)
    far_c = nb + lax.div(far_l, ROWS) * per_pair + lax.rem(far_l, per_pair)
    at_near = jnp.zeros((nb, lanes), F32)
    at_far = jnp.zeros((far, lanes), F32)
    for k in range(K):
        at_near += jnp.where(near_c == nbr[k : k + 1], coeff[k : k + 1], 0.0)
        at_far += jnp.where(far_c == nbr[k : k + 1], coeff[k : k + 1], 0.0)
    near_hi = at_near.astype(BF16).astype(F32)
    far_hi = at_far.astype(BF16).astype(F32)
    near_2 = jnp.concatenate([near_hi, at_near - near_hi], axis=0)
    far_2 = jnp.concatenate([far_hi, at_far - far_hi], axis=0)
    atn_bf[...] = near_2.astype(BF16)
    atf_bf[...] = far_2.astype(BF16)
    an_bf[...] = near_2.T.astype(BF16)
    far_t = far_2.T
    lane_2 = lax.broadcasted_iota(jnp.int32, (lanes, 2 * far), 1)
    lane_2g = lax.rem(lax.div(lane_2, per_pair), GROUPS)
    for g in range(GROUPS):
        af_bf[g] = jnp.where(lane_2g == g, far_t, 0.0).astype(BF16)

    for g in range(GROUPS):
        near[g] = dot(an_bf[...], jnp.concatenate([xk[g]] * 2, axis=0))

    wait_bytes(wbuf.at[dom, core, pl.ds(0, half - ROWS), :], phase_r.at[1])

    def ring_right(k):
        s = at_dom(-k)
        return copy_to(
            wbuf.at[s, core],
            wbuf.at[s, core],
            wring_s.at[0, k],
            wring_r.at[0, k],
            me,
            at_dom(1),
        )

    def ring_left(k):
        s = at_dom(k)
        return copy_to(
            wbuf.at[s, core],
            wbuf.at[s, core],
            wring_s.at[1, k],
            wring_r.at[1, k],
            me,
            at_dom(-1),
        )

    def pair(s, k):
        return copy_to(
            wbuf.at[s, core],
            wbuf.at[s, core],
            wpair_s.at[k],
            wpair_r.at[k],
            partner,
            dom,
        )

    def pass_on(k):
        if 1 <= k <= right:
            wait_bytes(wbuf.at[at_dom(-k), core], wring_r.at[0, k - 1])
        if k < right:
            ring_right(k).start()
        if 1 <= k <= left:
            wait_bytes(wbuf.at[at_dom(k), core], wring_r.at[1, k - 1])
        if k < left:
            ring_left(k).start()
        if k == 0:
            pair(dom, 0).start()
        else:
            pair(at_dom(-k), k).start()
            if k <= left:
                pair(at_dom(k), right + k).start()

    pass_on(0)

    wait_bytes(land.at[pl.ds(0, ny - 1)], phase_r.at[0])
    landed = land[...].reshape(far, width)
    landed = jnp.concatenate([landed] * 2, axis=0)
    for g in range(GROUPS):
        mix = (near[g] + dot(af_bf[g], landed)).astype(BF16)
        for i in range(group):
            f = g * group + i
            for t in range(NBANK):
                mixed[f * nb : (f + 1) * nb, t * TILE : (t + 1) * TILE] = mix[
                    t * nb : (t + 1) * nb, i * TILE : (i + 1) * TILE
                ]
    for g in range(GROUPS):
        rows = group * nb
        agg = lax.dot_general(
            mixed[g * rows : (g + 1) * rows, :],
            bank_u[...],
            NT,
            preferred_element_type=F32,
        )
        for i in range(group):
            shuf[pl.ds(g * group + i, nb, stride=ROWS), :] = agg[i * nb : (i + 1) * nb]
    send_a[...] = shuf[...].astype(BF16).reshape(nb, ROWS, TILE)

    def send_agg(step, carry):
        to = lax.rem(me + step, nf)
        copy_to(
            send_a.at[to], view.at[me], phase_s.at[2], phase_r.at[2], to, dom
        ).start()
        return carry

    lax.fori_loop(1, nf, send_agg, 0)
    view[me] = send_a[me]

    for k in range(1, right + 1):
        pass_on(k)

    wait_bytes(view.at[pl.ds(0, nf - 1)], phase_r.at[2])
    view_copy = copy_to(view, view2, phase_s.at[3], phase_r.at[3], partner, dom)
    view_copy.start()

    for k in range(ny):
        s = at_dom(-k) if k <= right else at_dom(k - right)
        wait_bytes(wbuf.at[s, 1 - core], wpair_r.at[k])

    rows_all = view[...].reshape(nf * ROWS, TILE)
    for c in range(2):
        pre = jnp.zeros((half, TILE), F32)
        for s in range(0, ny, 2):
            lhs = jnp.concatenate([wbuf[s, c], wbuf[s + 1, c]], axis=1)
            pre += dot(lhs, rows_all[s * chunk : (s + 2) * chunk])
        sig = jax.nn.sigmoid(pre)
        act_ref[:, c] = (pre * sig).astype(BF16).reshape(chips, ROWS, TILE)
        cot = cot_ref[:, c].reshape(half, TILE).astype(F32)
        slo = cot * (sig * (1.0 + pre * (1.0 - sig)))
        slo = slo.astype(BF16)
        slope[c] = slo
        slope_t[:, c * half : (c + 1) * half] = slo.astype(F32).T.astype(BF16)

    slope_copy = copy_to(
        slope.at[1 - core], slope2, phase_s.at[4], phase_r.at[4], partner, dom
    )
    slope_copy.start()

    for s in range(0, ny, 2):
        lhs = jnp.concatenate(
            [
                jnp.concatenate([wbuf[s, c], wbuf[s + 1, c]], axis=1)
                for c in range(2)
            ],
            axis=0,
        )
        grad = dot(slope_t[...], lhs).T
        send_g[s * per_chunk : (s + 2) * per_chunk] = grad.astype(BF16).reshape(
            2 * per_chunk, ROWS, TILE
        )

    def send_grad(step, carry):
        to = lax.rem(me + step, nf)
        copy_to(
            send_g.at[to], cols.at[me], phase_s.at[5], phase_r.at[5], to, dom
        ).start()
        return carry

    lax.fori_loop(1, nf, send_grad, 0)
    cols[me] = send_g[me]

    wait_bytes(view2, phase_r.at[3])
    wait_bytes(slope2, phase_r.at[4])
    own_slope = jnp.concatenate([slope[core], slope2[...]], axis=1)
    sub = half // SUB

    def partial(s):
        at = pl.ds(s * per_chunk, per_chunk)
        rhs = jnp.concatenate(
            [view[at].reshape(chunk, TILE), view2[at].reshape(chunk, TILE)], axis=1
        )
        return lax.dot_general(own_slope, rhs, NT, preferred_element_type=F32)

    def ring_copy(direction, k, h):
        src, dst = ((right_s, right_r), (left_s, left_r))[direction]
        at = pl.ds(h * sub, sub)
        return copy_to(
            src.at[k, at],
            dst.at[k, at],
            gring_s.at[direction, k, h],
            gring_r.at[direction, k, h],
            me,
            at_dom(1 - 2 * direction),
        )

    right_s[0] = partial(at_dom(right)).astype(BF16)
    for h in range(SUB):
        ring_copy(0, 0, h).start()
    left_s[0] = partial(at_dom(-left)).astype(BF16)
    for h in range(SUB):
        ring_copy(1, 0, h).start()
    for k in range(1, right):
        part[k - 1] = partial(at_dom(right - k))
    for k in range(1, left):
        part[right - 1 + k - 1] = partial(at_dom(k - left))
    part[ny - 3] = partial(dom)

    def ring_step(k):
        for h in range(SUB):
            at = pl.ds(h * sub, sub)
            if k < right:
                wait_bytes(right_r.at[k - 1, at], gring_r.at[0, k - 1, h])
                right_s[k, at] = (
                    part[k - 1, at] + right_r[k - 1, at].astype(F32)
                ).astype(BF16)
                ring_copy(0, k, h).start()
            if k < left:
                wait_bytes(left_r.at[k - 1, at], gring_r.at[1, k - 1, h])
                left_s[k, at] = (
                    part[right - 2 + k, at] + left_r[k - 1, at].astype(F32)
                ).astype(BF16)
                ring_copy(1, k, h).start()

    for k in range(1, right - 1):
        ring_step(k)

    wait_bytes(cols.at[pl.ds(0, nf - 1)], phase_r.at[5])
    shuf[...] = cols[...].reshape(nb * ROWS, TILE).astype(F32)
    for g in range(GROUPS):
        lhs = jnp.concatenate(
            [shuf[pl.ds(g * group + i, nb, stride=ROWS), :] for i in range(group)],
            axis=0,
        ).astype(BF16)
        mix = dot(lhs, bank_u[...]).astype(BF16)
        for i in range(group):
            for t in range(NBANK):
                back[g, t * nb : (t + 1) * nb, i * TILE : (i + 1) * TILE] = mix[
                    i * nb : (i + 1) * nb, t * TILE : (t + 1) * TILE
                ]
    far_rows = lax.broadcasted_iota(jnp.int32, (far, width), 0)
    far_g = lax.rem(lax.div(far_rows, per_pair), GROUPS)
    sent = jnp.zeros((far, width), F32)
    for g in range(GROUPS):
        both = dot(atf_bf[...], back[g])
        sent = jnp.where(far_g == g, both[:far] + both[far:], sent)
    send_d[...] = sent.astype(BF16).reshape(ny, ROWS, width)

    def send_back(step, carry):
        to = at_dom(step)
        copy_to(
            send_d.at[to], land_d.at[dom], phase_s.at[6], phase_r.at[6], me, to
        ).start()
        return carry

    lax.fori_loop(1, ny, send_back, 0)
    land_d[dom] = send_d[dom]
    for g in range(GROUPS):
        both = dot(atn_bf[...], back[g])
        own[g] = both[:nb] + both[nb:]

    ring_step(right - 1)

    wait_bytes(land_d.at[pl.ds(0, ny - 1)], phase_r.at[6])
    landed = land_d[...].reshape(far, width)
    for g in range(GROUPS):
        total = own[g] + dot(oht_bf[g], landed)
        for i in range(group):
            shuf[pl.ds(g * group + i, nb, stride=ROWS), :] = total[
                :, i * TILE : (i + 1) * TILE
            ]
    for b in range(nb):
        fg_ref[:, b * TILE : (b + 1) * TILE] = shuf[
            b * ROWS : (b + 1) * ROWS, :
        ].astype(BF16)

    for h in range(SUB):
        at = pl.ds(h * sub, sub)
        wait_bytes(right_r.at[right - 1, at], gring_r.at[0, right - 1, h])
        wait_bytes(left_r.at[left - 1, at], gring_r.at[1, left - 1, h])
        tiles = sub // ROWS
        send_z[h * tiles : (h + 1) * tiles] = (
            (
                part[ny - 3, at]
                + right_r[right - 1, at].astype(F32)
                + left_r[left - 1, at].astype(F32)
            )
            .astype(BF16)
            .reshape(tiles, ROWS, chunk)
        )

    def send_rows(step, carry):
        to = lax.rem(chip + step, chips)
        copy_to(
            send_z.at[to],
            land_z.at[chip],
            phase_s.at[7],
            phase_r.at[7],
            2 * to + core,
            dom,
        ).start()
        return carry

    lax.fori_loop(1, chips, send_rows, 0)
    land_z[chip] = send_z[chip]
    wait_bytes(land_z.at[pl.ds(0, chips - 1)], phase_r.at[7])
    rows_sum = land_z[0].astype(F32)
    for m in range(1, chips):
        rows_sum += land_z[m].astype(F32)
    send_y[...] = rows_sum * scale

    def send_out(step, carry):
        to = at_dom(step)
        copy_to(send_y, land_y.at[dom], phase_s.at[8], phase_r.at[8], me, to).start()
        return carry

    lax.fori_loop(1, ny, send_out, 0)
    land_y[dom] = send_y[...]
    wait_bytes(land_y.at[pl.ds(0, ny - 1)], phase_r.at[8])
    for s in range(ny):
        wg_ref[:, s * chunk : (s + 1) * chunk] = land_y[s]

    wait_bytes(out_blocks.at[pl.ds(0, ny - 1)], phase_s.at[0])
    wait_bytes(wbuf.at[0, 0, pl.ds(0, half - ROWS), :], phase_s.at[1])
    wait_bytes(send_a.at[pl.ds(0, nf - 1)], phase_s.at[2])
    view_copy.wait_send()
    slope_copy.wait_send()
    wait_bytes(send_g.at[pl.ds(0, nf - 1)], phase_s.at[5])
    wait_bytes(send_d.at[pl.ds(0, ny - 1)], phase_s.at[6])
    wait_bytes(send_z.at[pl.ds(0, chips - 1)], phase_s.at[7])
    wait_bytes(land_y.at[pl.ds(0, ny - 1)], phase_s.at[8])
    for k in range(right):
        ring_right(k).wait_send()
        for h in range(SUB):
            ring_copy(0, k, h).wait_send()
    for k in range(left):
        ring_left(k).wait_send()
        for h in range(SUB):
            ring_copy(1, k, h).wait_send()
    for k in range(ny):
        pair(dom, k).wait_send()


def per_device(
    nf,
    ny,
    features,
    weight,
    tile_bank,
    neighbors,
    tile_ids,
    edge_weight,
    counts,
    boundary,
    cotangent,
):
    nb = features.shape[2] // TILE
    per_pair = boundary.shape[2]
    chips = nf // 2
    half = chips * ROWS
    chunk = nf * ROWS // ny
    far = ny * ROWS
    lanes = NBANK * nb
    width = ROWS // GROUPS * TILE
    right = ny // 2
    left = ny - 1 - right
    scale = 1.0 / math.sqrt(ny * features.shape[2])
    vmem = pl.BlockSpec(memory_space=pltpu.VMEM)
    dma = pltpu.SemaphoreType.DMA
    act, feature_grad, weight_grad = pl.pallas_call(
        functools.partial(kernel, nf, ny, per_pair, scale),
        out_shape=(
            jax.ShapeDtypeStruct((chips, 2, ROWS, TILE), BF16),
            jax.ShapeDtypeStruct((ROWS, nb * TILE), BF16),
            jax.ShapeDtypeStruct((ROWS, nf * ROWS), F32),
        ),
        in_specs=[pl.BlockSpec(memory_space=pltpu.SMEM)] + [vmem] * 8,
        out_specs=(vmem, vmem, vmem),
        scratch_shapes=[
            pltpu.VMEM((nb * ROWS, TILE), F32),
            pltpu.VMEM((GROUPS, nb, width), BF16),
            pltpu.VMEM((ny, ROWS, width), BF16),
            pltpu.VMEM((ny, ROWS, width), BF16),
            pltpu.VMEM((GROUPS, lanes, width), F32),
            pltpu.VMEM((lanes, 2 * nb), BF16),
            pltpu.VMEM((GROUPS, lanes, 2 * far), BF16),
            pltpu.VMEM((2 * nb, lanes), BF16),
            pltpu.VMEM((2 * far, lanes), BF16),
            pltpu.VMEM((GROUPS, nb, far), BF16),
            pltpu.VMEM((TILE, NBANK * TILE), BF16),
            pltpu.VMEM((ROWS * nb, NBANK * TILE), BF16),
            pltpu.VMEM((nb, ROWS, TILE), BF16),
            pltpu.VMEM((nf, ROWS, TILE), BF16),
            pltpu.VMEM((nf, ROWS, TILE), BF16),
            pltpu.VMEM((ny, 2, half, chunk), BF16),
            pltpu.VMEM((2, half, TILE), BF16),
            pltpu.VMEM((TILE, 2 * half), BF16),
            pltpu.VMEM((half, TILE), BF16),
            pltpu.VMEM((nf, ROWS, TILE), BF16),
            pltpu.VMEM((nf, ROWS, TILE), BF16),
            pltpu.VMEM((GROUPS, lanes, width), BF16),
            pltpu.VMEM((GROUPS, nb, width), F32),
            pltpu.VMEM((ny, ROWS, width), BF16),
            pltpu.VMEM((ny, ROWS, width), BF16),
            pltpu.VMEM((ny - 2, half, chunk), F32),
            pltpu.VMEM((right, half, chunk), BF16),
            pltpu.VMEM((right, half, chunk), BF16),
            pltpu.VMEM((left, half, chunk), BF16),
            pltpu.VMEM((left, half, chunk), BF16),
            pltpu.VMEM((chips, ROWS, chunk), BF16),
            pltpu.VMEM((chips, ROWS, chunk), BF16),
            pltpu.VMEM((ROWS, chunk), F32),
            pltpu.VMEM((ny, ROWS, chunk), F32),
            dma((9,)),
            dma((9,)),
            dma((2, right)),
            dma((2, right)),
            dma((ny,)),
            dma((ny,)),
            dma((2, right, SUB)),
            dma((2, right, SUB)),
        ],
        compiler_params=pltpu.CompilerParams(
            collective_id=0,
            has_side_effects=True,
            vmem_limit_bytes=48 * 2**20,
        ),
    )(
        boundary[:, 0, :].T,
        features[0],
        weight,
        tile_bank,
        neighbors[0].T,
        tile_ids[0].T,
        edge_weight[0].T,
        counts,
        cotangent[0].reshape(chips, 2, ROWS, TILE),
    )
    return (
        act.reshape(cotangent.shape),
        feature_grad[None],
        weight_grad,
    )


def solution(mesh):
    in_specs = (
        P("dom", "feat", None),
        P("feat", None),
        P(),
        P("dom", None, None),
        P("dom", None, None),
        P("dom", None, None),
        P("dom", None),
        P(None, "dom", None),
        P("dom", None, "feat"),
    )
    out_specs = (P("dom", None, "feat"), P("dom", "feat", None), P("feat", None))
    return jax.shard_map(
        functools.partial(per_device, mesh.shape["feat"], mesh.shape["dom"]),
        mesh=mesh,
        in_specs=in_specs,
        out_specs=out_specs,
        check_vma=False,
    )
```

time: 294 us -> 83.9 us (0.29)
  waiting for transfers between devices: 142 us -> 0 us
  Pallas kernels: 0 us -> 75.2 us
  other arithmetic: 46.6 us -> 0 us
  starting transfers between devices: 35.4 us -> 0 us
  blocking collectives: 29.7 us -> 0 us
  between operations: 14.3 us -> 0.68 us
  matrix products: 8.89 us -> 0 us
  local copies, waits for them, and re-layouts: 15.4 us -> 6.97 us
    pallas_call x0 -> x1, Pallas kernels: none -> 75.2 us  [per_device(): pl.pallas_call(functools.partial(kernel, nf, ny, per_pair, scale), out_sh...]
    reduce_scatter x1 -> x0, waiting for transfers between devices: 64.2 us -> none  [per_device(): lax.psum_scatter(lax.dot_general(slope_bf, row_view, (((1,), (1,)), ((),...]
    scatter-add x2 -> x0, other arithmetic: 41.9 us -> none  [the longest x1 40.2 us: per_device(): jax.ops.segment_sum(edge_grad.reshape(block_count * K, slices, TILE), lin...]
    all_gather x1 -> x0, waiting for transfers between devices: 40.5 us -> none  [per_device(): full_weight = lax.all_gather(weight, 'feat', axis=0, tiled=True)]
    all_to_all x4 -> x0, waiting for transfers between devices: 36.9 us -> none  [the longest x1 11.9 us: per_device(): lax.all_to_all(aggregated, 'feat', split_axis=1, concat_axis=0, tiled=True)]
    all_to_all x4 -> x0, starting transfers between devices: 35.3 us -> none  [the longest x1 13.8 us: per_device(): lax.all_to_all(aggregated, 'feat', split_axis=1, concat_axis=0, tiled=True)]
    psum x1 -> x0, blocking collectives: 29.7 us -> none  [per_device(): lax.psum(feat_grad.astype(jnp.bfloat16), 'dom').astype(jnp.float32)]
    dot_general x7 -> x0, matrix products: 8.89 us -> none  [the longest x1 2.72 us: per_device(): lax.dot_general(slope_bf, row_view, (((1,), (1,)), ((), ())), preferred_e...]
  transfers between devices with their start and end apart: 6 -> 0, of which waited for: 6 -> 0; matrix products, arithmetic and copies ran while one was open for 21% -> 0% of each run, Pallas kernels for 0% -> 0%
where the time goes in v1:
time: 83.9 us; the launch traced here: 82.8 us
  Pallas kernels  75.2 us (90%)
  local copies, waits for them, and re-layouts  6.97 us (8%)
    pallas_call x1, Pallas kernels, per_device(): pl.pallas_call(functools.partial(kernel, nf, ny, per_pair, scale), out_sh...  75.2 us
    unnamed x21, local copies, waits for them, and re-layouts  6.97 us

profile of v1, /device:TPU:6, one launch (start us, length us, event | category | flops | bytes accessed | tf_op | source)
XLA Modules:
  0.0 82.8 jit_solution(14167555336777163166)
XLA Ops:
  0.6 0.0 copy-start.6
  0.6 0.0 copy-start.5
  0.7 0.0 copy-start.4
  0.7 0.0 copy-start.8
  0.7 0.6 copy-done.6
  1.3 0.0 copy-done.5
  1.3 0.0 copy-done.4
  1.4 0.0 copy-done.8
  1.4 0.0 copy-start
  1.4 0.9 %copy-done = bf16[1,16,8192]{2,1,0:T(8,128)(2,1)S(1)} copy-done((bf16[1,16,8192]{2,1,0:T(8,128)(2,1)S(1)}, bf16[1,16,8192]{2,1,0:T(8,128)(2,1)}, u32[]{:S(2)}) %copy-start) | copy-done | bytes 262168
  2.3 0.0 copy-start.1
  2.3 0.9 %copy-done.1 = bf16[1,1024,128]{2,1,0:T(8,128)(2,1)S(1)} copy-done((bf16[1,1024,128]{2,1,0:T(8,128)(2,1)S(1)}, bf16[1,1024,128]{2,1,0:T(8,128)(2,1)}, u32[]{:S(2)}) %copy-start.1) | copy-done | bytes 262168
  3.3 0.0 copy-start.2
  3.3 0.9 %copy-done.2 = bf16[4,128,128]{2,1,0:T(8,128)(2,1)S(1)} copy-done((bf16[4,128,128]{2,1,0:T(8,128)(2,1)S(1)}, bf16[4,128,128]{2,1,0:T(8,128)(2,1)}, u32[]{:S(2)}) %copy-start.2) | copy-done | bytes 131096
  4.2 0.0 copy-start.3
  4.2 0.8 copy-done.3
  4.9 0.0 copy-start.7
  4.9 0.7 copy-done.7
  5.6 75.2 %shard_map.112 = (bf16[32,2,16,128]{3,2,1,0:T(8,128)(2,1)S(1)}, bf16[16,8192]{1,0:T(8,128)(2,1)S(1)}, f32[16,1024]{1,0:T(8,128)S(1)}) custom-call(s32[4,8]{1,0:T(4,128)S(1)} %bitcast.22, bf16[16,8192]{1,0:T(8,128)(2,1)S(1)} %bitcast.16, bf16[16,1024]{1,0:T(8,128)(2,1)S(1)} %copy-done.3, bf16[4,128,128]{2,1,0:T(8,128)(2,1)S(1)} %copy-done.2, ...), custom_call_target="tpu_custom_call" | custom-call | tf_op jit(solution)/shard_map/pallas_call | solution.py:569
  80.8 0.7 copy.15
  81.5 0.7 copy.16
  82.2 0.6 copy.17
Async XLA Ops:
  0.6 0.7 copy-start.6
  0.6 0.7 copy-start.5
  0.7 0.7 copy-start.4
  0.7 0.7 copy-start.8
  1.4 1.0 %copy-start = (bf16[1,16,8192]{2,1,0:T(8,128)(2,1)S(1)}, bf16[1,16,8192]{2,1,0:T(8,128)(2,1)}, u32[]{:S(2)}) copy-start(bf16[1,16,8192]{2,1,0:T(8,128)(2,1)} %param.9) | copy-start | bytes 786436
  2.3 0.9 %copy-start.1 = (bf16[1,1024,128]{2,1,0:T(8,128)(2,1)S(1)}, bf16[1,1024,128]{2,1,0:T(8,128)(2,1)}, u32[]{:S(2)}) copy-start(bf16[1,1024,128]{2,1,0:T(8,128)(2,1)} %param.17) | copy-start | bytes 786436
  3.3 0.9 %copy-start.2 = (bf16[4,128,128]{2,1,0:T(8,128)(2,1)S(1)}, bf16[4,128,128]{2,1,0:T(8,128)(2,1)}, u32[]{:S(2)}) copy-start(bf16[4,128,128]{2,1,0:T(8,128)(2,1)} %bank_ref.1) | copy-start | bytes 393220
  4.2 0.8 copy-start.3
  4.9 0.7 copy-start.7

commit v2 on v1

v2 whole, which is shorter than its diff:
```python
import functools
import math

import jax
import jax.numpy as jnp
from jax import lax
from jax.experimental import pallas as pl
from jax.experimental.pallas import tpu as pltpu
from jax.sharding import PartitionSpec as P

TILE = 128
NBANK = 4
K = 8
ROWS = 16
GROUPS = 4
MESH = pl.DeviceIdType.MESH
F32 = jnp.float32
BF16 = jnp.bfloat16
NX = 4

NT = (((1,), (1,)), ((), ()))


def dot(a, b):
    return jnp.dot(a, b, preferred_element_type=F32)


def kernel(
    nf,
    ny,
    per_pair,
    scale,
    bnd_hbm,
    x_hbm,
    w_hbm,
    bank_hbm,
    nbr_hbm,
    tid_hbm,
    ew_hbm,
    cnt_hbm,
    cot_hbm,
    act_hbm,
    fg_hbm,
    wg_hbm,
    act_ref,
    fg_ref,
    wg_ref,
    bnd_ref,
    x_ref,
    bank_ref,
    nbr_ref,
    tid_ref,
    ew_ref,
    cnt_ref,
    cot_ref,
    shuf,
    xk,
    out_blocks,
    land,
    near,
    an_bf,
    af_bf,
    atn_bf,
    atf_bf,
    oht_bf,
    bank_u,
    mixed,
    send_a,
    view,
    view2,
    wbuf,
    slope,
    slope_t,
    slope2,
    send_g,
    cols,
    back,
    own,
    send_d,
    land_d,
    send_x,
    land_x,
    send_z,
    land_z,
    send_y,
    land_y,
    in_sem,
    go_sem,
    phase_s,
    phase_r,
    wz_s,
    wz_r,
    wx_s,
    wx_r,
    wp_s,
    wp_r,
    gx_s,
    gx_r,
):
    nb = nf
    nx = NX
    nz = nf // (2 * nx)
    chips = nf // 2
    chunk = nf * ROWS // ny
    per_chunk = chunk // ROWS
    half = chips * ROWS
    far = ny * ROWS
    lanes = NBANK * nb
    group = ROWS // GROUPS
    width = group * TILE

    me = lax.axis_index("feat")
    dom = lax.axis_index("dom")
    core = lax.rem(me, 2)
    col = lax.rem(lax.div(me, 2), nx)
    row = lax.div(me, 2 * nx)
    partner = me + 1 - 2 * core

    def device(z, x, c):
        return (z * nx + x) * 2 + c

    def at_dom(step):
        return lax.rem(dom + step + ny, ny)

    def at_row(step):
        return lax.rem(row + step + nz, nz)

    def at_col(step):
        return lax.rem(col + step + nx, nx)

    def copy_to(src, dst, send_sem, recv_sem, feat_id, dom_id):
        return pltpu.make_async_remote_copy(
            src_ref=src,
            dst_ref=dst,
            send_sem=send_sem,
            recv_sem=recv_sem,
            device_id=(feat_id, dom_id),
            device_id_type=MESH,
        )

    def wait_bytes(ref, sem):
        pltpu.make_async_copy(ref, ref, sem).wait()

    barrier = pltpu.get_barrier_semaphore()

    def greet(feat_id, dom_id):
        pl.semaphore_signal(
            barrier, inc=1, device_id=(feat_id, dom_id), device_id_type=MESH
        )

    for step in range(1, ny):
        greet(me, at_dom(step))
    for step in range(1, nz):
        greet(device(at_row(step), col, core), dom)
    for step in range(1, 2 * nx):
        greet(row * (2 * nx) + lax.rem(lax.rem(me, 2 * nx) + step, 2 * nx), dom)

    fetches = [
        pltpu.make_async_copy(src, dst, in_sem.at[i])
        for i, (src, dst) in enumerate(
            (
                (x_hbm, x_ref),
                (bnd_hbm, bnd_ref),
                (w_hbm, wbuf.at[core, row, col]),
                (nbr_hbm, nbr_ref),
                (tid_hbm, tid_ref),
                (ew_hbm, ew_ref),
                (cnt_hbm, cnt_ref),
                (bank_hbm, bank_ref),
                (cot_hbm, cot_ref),
            )
        )
    ]
    for fetch in fetches:
        fetch.start()
    for fetch in fetches[:3]:
        fetch.wait()

    for b in range(nb):
        shuf[b * ROWS : (b + 1) * ROWS, :] = x_ref[
            :, b * TILE : (b + 1) * TILE
        ].astype(F32)
    for f in range(ROWS):
        xk[f // group, :, (f % group) * TILE : (f % group + 1) * TILE] = shuf[
            pl.ds(f, nb, stride=ROWS), :
        ].astype(BF16)

    lane = lax.broadcasted_iota(jnp.int32, (per_pair, far), 1)
    spread = jnp.full((per_pair, far), -1, jnp.int32)
    for q in range(ny):
        spread = jnp.where(
            lax.div(lane, ROWS) == q, bnd_ref[:, q : q + 1], spread
        )
    lane = lax.broadcasted_iota(jnp.int32, (1, far), 1)
    lane_g = lax.rem(lax.div(lane, per_pair), GROUPS)
    lane_j = lax.rem(lane, per_pair)
    wanted = spread[0:1]
    for j in range(1, per_pair):
        wanted = jnp.where(lane_j == j, spread[j : j + 1], wanted)
    row_b = lax.broadcasted_iota(jnp.int32, (nb, far), 0)
    hots = [
        jnp.where((row_b == wanted) & (lane_g == g), 1.0, 0.0) for g in range(GROUPS)
    ]
    for g in range(GROUPS):
        oht_bf[g] = hots[g].astype(BF16)
    hot = jnp.concatenate(hots, axis=0).T.astype(BF16)
    out_blocks[...] = (
        dot(hot, xk[...].reshape(GROUPS * nb, width))
        .astype(BF16)
        .reshape(ny, ROWS, width)
    )

    pl.semaphore_wait(barrier, ny - 1 + nz - 1 + 2 * nx - 1)

    for step in range(1, nz):
        pl.semaphore_signal(
            go_sem,
            inc=1,
            device_id=(device(at_row(step), col, core), dom),
            device_id_type=MESH,
        )

    for step in range(1, ny):
        to = at_dom(step)
        copy_to(
            out_blocks.at[to], land.at[dom], phase_s.at[0], phase_r.at[0], me, to
        ).start()

    def weight_z(step):
        block = wbuf.at[core, row, col]
        return copy_to(
            block,
            block,
            wz_s.at[step],
            wz_r.at[step],
            device(at_row(step), col, core),
            dom,
        )

    def weight_x(step, aside):
        block = wbuf.at[core, at_row(-step), col]
        return copy_to(
            block,
            block,
            wx_s.at[step],
            wx_r.at[step],
            device(row, at_col(aside), core),
            dom,
        )

    def weight_pair(step):
        blocks = wbuf.at[core, at_row(-step)]
        return copy_to(blocks, blocks, wp_s.at[step], wp_r.at[step], partner, dom)

    order = [0]
    for step in range(1, nz // 2 + 1):
        order.append(step)
        if nz - step != step:
            order.append(nz - step)

    def forward_x(step):
        if step:
            wait_bytes(wbuf.at[core, at_row(-step), col], wz_r.at[step])
        for aside in range(1, nx):
            weight_x(step, aside).start()

    def forward_pair(step):
        wait_bytes(wbuf.at[core, at_row(-step), pl.ds(0, nx - 1)], wx_r.at[step])
        weight_pair(step).start()

    forward_x(0)
    for step in order[1:]:
        weight_z(step).start()
    land[dom] = out_blocks[dom]

    for fetch in fetches[3:]:
        fetch.wait()
    for t in range(NBANK):
        bank_u[:, t * TILE : (t + 1) * TILE] = bank_ref[t]
    nbr = jnp.concatenate([nbr_ref[...]] * NBANK, axis=1)
    tid = jnp.concatenate([tid_ref[...]] * NBANK, axis=1)
    edge = jnp.concatenate([ew_ref[...].astype(F32)] * NBANK, axis=1)
    cnt = jnp.concatenate([cnt_ref[...]] * NBANK, axis=1)
    lane_t = lax.div(lax.broadcasted_iota(jnp.int32, (K, lanes), 1), nb)
    slot = lax.broadcasted_iota(jnp.int32, (K, lanes), 0)
    coeff = jnp.where((tid == lane_t) & (slot < cnt), edge, 0.0)
    near_c = lax.broadcasted_iota(jnp.int32, (nb, lanes), 0)
    far_l = lax.broadcasted_iota(jnp.int32, (far, lanes), 0)
    far_c = nb + lax.div(far_l, ROWS) * per_pair + lax.rem(far_l, per_pair)
    at_near = jnp.zeros((nb, lanes), F32)
    at_far = jnp.zeros((far, lanes), F32)
    for k in range(K):
        at_near += jnp.where(near_c == nbr[k : k + 1], coeff[k : k + 1], 0.0)
        at_far += jnp.where(far_c == nbr[k : k + 1], coeff[k : k + 1], 0.0)
    near_hi = at_near.astype(BF16).astype(F32)
    far_hi = at_far.astype(BF16).astype(F32)
    near_2 = jnp.concatenate([near_hi, at_near - near_hi], axis=0)
    far_2 = jnp.concatenate([far_hi, at_far - far_hi], axis=0)
    atn_bf[...] = near_2.astype(BF16)
    atf_bf[...] = far_2.astype(BF16)
    an_bf[...] = near_2.T.astype(BF16)
    far_t = far_2.T
    lane_2 = lax.broadcasted_iota(jnp.int32, (lanes, 2 * far), 1)
    lane_2g = lax.rem(lax.div(lane_2, per_pair), GROUPS)
    for g in range(GROUPS):
        af_bf[g] = jnp.where(lane_2g == g, far_t, 0.0).astype(BF16)

    for g in range(GROUPS):
        near[g] = dot(an_bf[...], jnp.concatenate([xk[g]] * 2, axis=0))

    for step in order[1:3]:
        forward_x(step)

    wait_bytes(land.at[pl.ds(0, ny - 1)], phase_r.at[0])
    landed = land[...].reshape(far, width)
    landed = jnp.concatenate([landed] * 2, axis=0)
    for g in range(GROUPS):
        mix = (near[g] + dot(af_bf[g], landed)).astype(BF16)
        for i in range(group):
            f = g * group + i
            for t in range(NBANK):
                mixed[f * nb : (f + 1) * nb, t * TILE : (t + 1) * TILE] = mix[
                    t * nb : (t + 1) * nb, i * TILE : (i + 1) * TILE
                ]
    for g in range(GROUPS):
        rows = group * nb
        agg = lax.dot_general(
            mixed[g * rows : (g + 1) * rows, :],
            bank_u[...],
            NT,
            preferred_element_type=F32,
        )
        for i in range(group):
            shuf[pl.ds(g * group + i, nb, stride=ROWS), :] = agg[i * nb : (i + 1) * nb]
    send_a[...] = shuf[...].astype(BF16).reshape(nb, ROWS, TILE)

    pl.semaphore_wait(go_sem, nz - 1)

    def send_agg(step, carry):
        to = lax.rem(me + step, nf)
        copy_to(
            send_a.at[to], view.at[me], phase_s.at[1], phase_r.at[1], to, dom
        ).start()
        return carry

    lax.fori_loop(1, nf, send_agg, 0)
    view[me] = send_a[me]

    for step in order[3:]:
        forward_x(step)
    for step in order:
        forward_pair(step)

    wait_bytes(view.at[pl.ds(0, nf - 1)], phase_r.at[1])
    view_copy = copy_to(view, view2, phase_s.at[2], phase_r.at[2], partner, dom)
    view_copy.start()

    rows_all = view[...].reshape(nf * ROWS, TILE)
    for turn in range(2):
        c = core if turn == 0 else 1 - core
        if turn == 1:
            for step in order:
                wait_bytes(wbuf.at[1 - core, at_row(-step)], wp_r.at[step])
        pre = dot(wbuf[c].reshape(half, nf * ROWS), rows_all)
        sig = jax.nn.sigmoid(pre)
        act_ref[:, c] = (pre * sig).astype(BF16).reshape(chips, ROWS, TILE)
        cot = cot_ref[:, c].reshape(half, TILE).astype(F32)
        slo = cot * (sig * (1.0 + pre * (1.0 - sig)))
        slo = slo.astype(BF16)
        slope[c] = slo

    slope_copy = copy_to(
        slope.at[1 - core], slope2, phase_s.at[3], phase_r.at[3], partner, dom
    )
    slope_copy.start()
    act_out = pltpu.make_async_copy(act_ref, act_hbm, in_sem.at[9])
    act_out.start()

    for c in range(2):
        slope_t[:, c * half : (c + 1) * half] = slope[c].astype(F32).T.astype(BF16)
    piece = 2 * chunk
    for s in range(0, ny, 2):
        at = slice(s * chunk, (s + 2) * chunk)
        lhs = jnp.concatenate(
            [wbuf[c, :, :, :, at].reshape(half, piece) for c in range(2)], axis=0
        )
        grad = dot(slope_t[...], lhs).T
        send_g[s * per_chunk : (s + 2) * per_chunk] = grad.astype(BF16).reshape(
            2 * per_chunk, ROWS, TILE
        )

    def send_grad(step, carry):
        to = lax.rem(me + step, nf)
        copy_to(
            send_g.at[to], cols.at[me], phase_s.at[4], phase_r.at[4], to, dom
        ).start()
        return carry

    lax.fori_loop(1, nf, send_grad, 0)
    cols[me] = send_g[me]

    wait_bytes(view2, phase_r.at[2])
    wait_bytes(slope2, phase_r.at[3])
    own_slope = jnp.concatenate([slope[core], slope2[...]], axis=1)

    def partial_x(k, aside):
        to = at_col(aside)
        return copy_to(
            send_x.at[k, to],
            land_x.at[k, aside - 1],
            gx_s.at[k],
            gx_r.at[k],
            device(row, to, core),
            dom,
        )

    for k in range(ny):
        at = pl.ds(at_dom(k) * per_chunk, per_chunk)
        rhs = jnp.concatenate(
            [view[at].reshape(chunk, TILE), view2[at].reshape(chunk, TILE)], axis=1
        )
        part = lax.dot_general(own_slope, rhs, NT, preferred_element_type=F32)
        part = part.astype(BF16).reshape(nz, nx, ROWS, chunk)
        for x in range(nx):
            send_x[k, x] = part[:, x]
        for aside in range(1, nx):
            partial_x(k, aside).start()

    def spread_out(k):
        to = at_dom(k)
        wait_bytes(land_x.at[k], gx_r.at[k])
        total = send_x[k, col].astype(F32)
        for aside in range(1, nx):
            total += land_x[k, aside - 1].astype(F32)
        send_z[k] = total.astype(BF16)
        for step in range(nz):
            if k == 0 and step == 0:
                continue
            z = at_row(step)
            copy_to(
                send_z.at[k, z],
                land_z.at[row * ny + dom],
                phase_s.at[5],
                phase_r.at[5],
                device(z, col, core),
                to,
            ).start()

    for k in range(ny // 2):
        spread_out(k)

    wait_bytes(cols.at[pl.ds(0, nf - 1)], phase_r.at[4])
    shuf[...] = cols[...].reshape(nb * ROWS, TILE).astype(F32)
    for g in range(GROUPS):
        lhs = jnp.concatenate(
            [shuf[pl.ds(g * group + i, nb, stride=ROWS), :] for i in range(group)],
            axis=0,
        ).astype(BF16)
        mix = dot(lhs, bank_u[...]).astype(BF16)
        for i in range(group):
            for t in range(NBANK):
                back[g, t * nb : (t + 1) * nb, i * TILE : (i + 1) * TILE] = mix[
                    i * nb : (i + 1) * nb, t * TILE : (t + 1) * TILE
                ]
    far_rows = lax.broadcasted_iota(jnp.int32, (far, width), 0)
    far_g = lax.rem(lax.div(far_rows, per_pair), GROUPS)
    sent = jnp.zeros((far, width), F32)
    for g in range(GROUPS):
        both = dot(atf_bf[...], back[g])
        sent = jnp.where(far_g == g, both[:far] + both[far:], sent)
    send_d[...] = sent.astype(BF16).reshape(ny, ROWS, width)

    for step in range(1, ny):
        to = at_dom(step)
        copy_to(
            send_d.at[to], land_d.at[dom], phase_s.at[6], phase_r.at[6], me, to
        ).start()
    land_d[dom] = send_d[dom]

    for k in range(ny // 2, ny):
        spread_out(k)
    land_z[row * ny + dom] = send_z[0, row]

    for g in range(GROUPS):
        both = dot(atn_bf[...], back[g])
        own[g] = both[:nb] + both[nb:]

    wait_bytes(land_d.at[pl.ds(0, ny - 1)], phase_r.at[6])
    landed = land_d[...].reshape(far, width)
    for g in range(GROUPS):
        total = own[g] + dot(oht_bf[g], landed)
        for i in range(group):
            shuf[pl.ds(g * group + i, nb, stride=ROWS), :] = total[
                :, i * TILE : (i + 1) * TILE
            ]
    for b in range(nb):
        fg_ref[:, b * TILE : (b + 1) * TILE] = shuf[
            b * ROWS : (b + 1) * ROWS, :
        ].astype(BF16)

    fg_out = pltpu.make_async_copy(fg_ref, fg_hbm, in_sem.at[10])
    fg_out.start()

    wait_bytes(land_z.at[pl.ds(0, nz * ny - 1)], phase_r.at[5])
    rows_sum = land_z[0].astype(F32)
    for m in range(1, nz * ny):
        rows_sum += land_z[m].astype(F32)
    send_y[...] = rows_sum * scale
    for step in range(1, ny):
        to = at_dom(step)
        copy_to(send_y, land_y.at[dom], phase_s.at[7], phase_r.at[7], me, to).start()
    land_y[dom] = send_y[...]

    wait_bytes(out_blocks.at[pl.ds(0, ny - 1)], phase_s.at[0])
    wait_bytes(send_a.at[pl.ds(0, nf - 1)], phase_s.at[1])
    view_copy.wait_send()
    slope_copy.wait_send()
    wait_bytes(send_g.at[pl.ds(0, nf - 1)], phase_s.at[4])
    wait_bytes(land_z.at[pl.ds(0, nz * ny - 1)], phase_s.at[5])
    wait_bytes(send_d.at[pl.ds(0, ny - 1)], phase_s.at[6])
    for step in order:
        if step:
            weight_z(step).wait_send()
        wait_bytes(wbuf.at[0, 0, pl.ds(0, nx - 1)], wx_s.at[step])
        weight_pair(step).wait_send()
    for k in range(ny):
        wait_bytes(land_x.at[k], gx_s.at[k])

    wait_bytes(land_y.at[pl.ds(0, ny - 1)], phase_r.at[7])
    for s in range(ny):
        wg_ref[:, s * chunk : (s + 1) * chunk] = land_y[s]
    wg_out = pltpu.make_async_copy(wg_ref, wg_hbm, in_sem.at[11])
    wg_out.start()
    act_out.wait()
    fg_out.wait()
    wg_out.wait()
    wait_bytes(land_y.at[pl.ds(0, ny - 1)], phase_s.at[7])


def per_device(
    nf,
    ny,
    features,
    weight,
    tile_bank,
    neighbors,
    tile_ids,
    edge_weight,
    counts,
    boundary,
    cotangent,
):
    nb = features.shape[2] // TILE
    per_pair = boundary.shape[2]
    nx = NX
    nz = nf // (2 * nx)
    chips = nf // 2
    half = chips * ROWS
    chunk = nf * ROWS // ny
    far = ny * ROWS
    lanes = NBANK * nb
    width = ROWS // GROUPS * TILE
    scale = 1.0 / math.sqrt(ny * features.shape[2])
    hbm = pl.BlockSpec(memory_space=pl.ANY)
    dma = pltpu.SemaphoreType.DMA
    act, feature_grad, weight_grad = pl.pallas_call(
        functools.partial(kernel, nf, ny, per_pair, scale),
        out_shape=(
            jax.ShapeDtypeStruct((chips, 2, ROWS, TILE), BF16),
            jax.ShapeDtypeStruct((ROWS, nb * TILE), BF16),
            jax.ShapeDtypeStruct((ROWS, nf * ROWS), F32),
        ),
        in_specs=[hbm] * 9,
        out_specs=(hbm, hbm, hbm),
        scratch_shapes=[
            pltpu.VMEM((chips, 2, ROWS, TILE), BF16),
            pltpu.VMEM((ROWS, nb * TILE), BF16),
            pltpu.VMEM((ROWS, nf * ROWS), F32),
            pltpu.VMEM((per_pair, ny), jnp.int32),
            pltpu.VMEM((ROWS, nb * TILE), BF16),
            pltpu.VMEM((NBANK, TILE, TILE), BF16),
            pltpu.VMEM((K, nb), jnp.int32),
            pltpu.VMEM((K, nb), jnp.int32),
            pltpu.VMEM((K, nb), BF16),
            pltpu.VMEM((1, nb), jnp.int32),
            pltpu.VMEM((chips, 2, ROWS, TILE), BF16),
            pltpu.VMEM((nb * ROWS, TILE), F32),
            pltpu.VMEM((GROUPS, nb, width), BF16),
            pltpu.VMEM((ny, ROWS, width), BF16),
            pltpu.VMEM((ny, ROWS, width), BF16),
            pltpu.VMEM((GROUPS, lanes, width), F32),
            pltpu.VMEM((lanes, 2 * nb), BF16),
            pltpu.VMEM((GROUPS, lanes, 2 * far), BF16),
            pltpu.VMEM((2 * nb, lanes), BF16),
            pltpu.VMEM((2 * far, lanes), BF16),
            pltpu.VMEM((GROUPS, nb, far), BF16),
            pltpu.VMEM((TILE, NBANK * TILE), BF16),
            pltpu.VMEM((ROWS * nb, NBANK * TILE), BF16),
            pltpu.VMEM((nb, ROWS, TILE), BF16),
            pltpu.VMEM((nf, ROWS, TILE), BF16),
            pltpu.VMEM((nf, ROWS, TILE), BF16),
            pltpu.VMEM((2, nz, nx, ROWS, nf * ROWS), BF16),
            pltpu.VMEM((2, half, TILE), BF16),
            pltpu.VMEM((TILE, 2 * half), BF16),
            pltpu.VMEM((half, TILE), BF16),
            pltpu.VMEM((nf, ROWS, TILE), BF16),
            pltpu.VMEM((nf, ROWS, TILE), BF16),
            pltpu.VMEM((GROUPS, lanes, width), BF16),
            pltpu.VMEM((GROUPS, nb, width), F32),
            pltpu.VMEM((ny, ROWS, width), BF16),
            pltpu.VMEM((ny, ROWS, width), BF16),
            pltpu.VMEM((ny, nx, nz, ROWS, chunk), BF16),
            pltpu.VMEM((ny, nx - 1, nz, ROWS, chunk), BF16),
            pltpu.VMEM((ny, nz, ROWS, chunk), BF16),
            pltpu.VMEM((nz * ny, ROWS, chunk), BF16),
            pltpu.VMEM((ROWS, chunk), F32),
            pltpu.VMEM((ny, ROWS, chunk), F32),
            dma((12,)),
            pltpu.SemaphoreType.REGULAR,
            dma((8,)),
            dma((8,)),
            dma((nz,)),
            dma((nz,)),
            dma((nz,)),
            dma((nz,)),
            dma((nz,)),
            dma((nz,)),
            dma((ny,)),
            dma((ny,)),
        ],
        compiler_params=pltpu.CompilerParams(
            collective_id=0,
            has_side_effects=True,
            vmem_limit_bytes=60 * 2**20,
        ),
    )(
        boundary[:, 0, :].T,
        features[0],
        weight,
        tile_bank,
        neighbors[0].T,
        tile_ids[0].T,
        edge_weight[0].T,
        counts,
        cotangent[0].reshape(chips, 2, ROWS, TILE),
    )
    return (
        act.reshape(cotangent.shape),
        feature_grad[None],
        weight_grad,
    )


def solution(mesh):
    in_specs = (
        P("dom", "feat", None),
        P("feat", None),
        P(),
        P("dom", None, None),
        P("dom", None, None),
        P("dom", None, None),
        P("dom", None),
        P(None, "dom", None),
        P("dom", None, "feat"),
    )
    out_specs = (P("dom", None, "feat"), P("dom", "feat", None), P("feat", None))
    return jax.shard_map(
        functools.partial(per_device, mesh.shape["feat"], mesh.shape["dom"]),
        mesh=mesh,
        in_specs=in_specs,
        out_specs=out_specs,
        check_vma=False,
    )
```

time: 83.9 us -> 70.6 us (0.84); the launches traced: 82.8 us -> 70.4 us
  Pallas kernels: 75.2 us -> 66.5 us
  local copies, waits for them, and re-layouts: 6.97 us -> 3.21 us
    pallas_call x1, Pallas kernels: 75.2 us -> 66.5 us  [per_device(): pl.pallas_call(functools.partial(kernel, nf, ny, per_pair, scale), out_sh...]
    unnamed x21 -> x7, local copies, waits for them, and re-layouts: 6.97 us -> 3.21 us
where the time goes in v2:
time: 70.6 us; the launch traced here: 70.4 us
  Pallas kernels  66.5 us (94%)
  local copies, waits for them, and re-layouts  3.21 us (5%)
    pallas_call x1, Pallas kernels, per_device(): pl.pallas_call(functools.partial(kernel, nf, ny, per_pair, scale), out_sh...  66.5 us
    unnamed x7, local copies, waits for them, and re-layouts  3.21 us

profile of v2, /device:TPU:6, one launch (start us, length us, event | category | flops | bytes accessed | tf_op | source)
XLA Modules:
  0.0 70.4 jit_solution(14429062476093091217)
XLA Ops:
  0.6 66.5 %shard_map.112 = (bf16[32,2,16,128]{3,2,1,0:T(8,128)(2,1)}, bf16[16,8192]{1,0:T(8,128)(2,1)}, f32[16,1024]{1,0:T(8,128)}) custom-call(s32[4,8]{1,0:T(4,128)} %bitcast.22, bf16[16,8192]{1,0:T(8,128)(2,1)} %bitcast.16, bf16[16,1024]{1,0:T(8,128)(2,1)} %w_hbm.1, bf16[4,128,128]{2,1,0:T(8,128)(2,1)} %bank_hbm.1, s32[8,64]{1,0:T(8,128)} %bitcast.20, ...), custom_call_target="tpu_custom_call" | custom-call | tf_op jit(solution)/shard_map/pallas_call | solution.py:566
  67.2 0.0 copy-start
  67.2 1.7 %copy.15 = bf16[1,1024,128]{2,1,0:T(8,128)(2,1)} copy(bf16[1,1024,128]{2,1,0:T(8,128)(2,1)} %bitcast.19) | data formatting | bytes 524288
  68.9 0.0 copy-done
  68.9 0.0 copy-start.1
  68.9 0.7 copy.16
  69.6 0.2 copy-done.1
  69.8 0.6 copy.17
Async XLA Ops:
  67.2 1.7 %copy-start = (bf16[16,8192]{1,0:T(8,128)(2,1)S(1)}, bf16[16,8192]{1,0:T(8,128)(2,1)}, u32[]{:S(2)}) copy-start(bf16[16,8192]{1,0:T(8,128)(2,1)} %get-tuple-element.7) | copy-start | bytes 786436
  68.9 0.9 %copy-start.1 = (f32[16,1024]{1,0:T(8,128)S(1)}, f32[16,1024]{1,0:T(8,128)}, u32[]{:S(2)}) copy-start(f32[16,1024]{1,0:T(8,128)} %get-tuple-element.14) | copy-start | bytes 196612

commit v3 on v2

--- a/solution.py
+++ b/solution.py
@@ -17,6 +17,9 @@
 F32 = jnp.float32
 BF16 = jnp.bfloat16
 NX = 4
+EARLY = 3
+MIDDLE = 5
+ZX = 4
 
 NT = (((1,), (1,)), ((), ()))
 
@@ -82,6 +85,13 @@
     land_x,
     send_z,
     land_z,
+    rest_of,
+    right_s,
+    right_r,
+    left_s,
+    left_r,
+    send_w,
+    land_w,
     send_y,
     land_y,
     in_sem,
@@ -96,6 +106,8 @@
     wp_r,
     gx_s,
     gx_r,
+    gr_s,
+    gr_r,
 ):
     nb = nf
     nx = NX
@@ -108,6 +120,12 @@
     lanes = NBANK * nb
     group = ROWS // GROUPS
     width = group * TILE
+    zx = ZX
+    zy = nz - zx
+    ring_tiles = zy * nx
+    ring_rows = ring_tiles * ROWS
+    right = ny // 2
+    left = ny - 1 - right
 
     me = lax.axis_index("feat")
     dom = lax.axis_index("dom")
@@ -308,7 +326,7 @@
     for g in range(GROUPS):
         near[g] = dot(an_bf[...], jnp.concatenate([xk[g]] * 2, axis=0))
 
-    for step in order[1:3]:
+    for step in order[1:EARLY]:
         forward_x(step)
 
     wait_bytes(land.at[pl.ds(0, ny - 1)], phase_r.at[0])
@@ -334,6 +352,8 @@
             shuf[pl.ds(g * group + i, nb, stride=ROWS), :] = agg[i * nb : (i + 1) * nb]
     send_a[...] = shuf[...].astype(BF16).reshape(nb, ROWS, TILE)
 
+    for step in order[EARLY:MIDDLE]:
+        forward_x(step)
     pl.semaphore_wait(go_sem, nz - 1)
 
     def send_agg(step, carry):
@@ -346,7 +366,7 @@
     lax.fori_loop(1, nf, send_agg, 0)
     view[me] = send_a[me]
 
-    for step in order[3:]:
+    for step in order[MIDDLE:]:
         forward_x(step)
     for step in order:
         forward_pair(step)
@@ -389,16 +409,6 @@
             2 * per_chunk, ROWS, TILE
         )
 
-    def send_grad(step, carry):
-        to = lax.rem(me + step, nf)
-        copy_to(
-            send_g.at[to], cols.at[me], phase_s.at[4], phase_r.at[4], to, dom
-        ).start()
-        return carry
-
-    lax.fori_loop(1, nf, send_grad, 0)
-    cols[me] = send_g[me]
-
     wait_bytes(view2, phase_r.at[2])
     wait_bytes(slope2, phase_r.at[3])
     own_slope = jnp.concatenate([slope[core], slope2[...]], axis=1)
@@ -414,17 +424,68 @@
             dom,
         )
 
-    for k in range(ny):
+    def send_grad(step, carry):
+        to = lax.rem(me + step, nf)
+        copy_to(
+            send_g.at[to], cols.at[me], phase_s.at[4], phase_r.at[4], to, dom
+        ).start()
+        return carry
+
+    lax.fori_loop(1, nf, send_grad, 0)
+    cols[me] = send_g[me]
+
+    def ring_copy(direction, k):
+        src, dst = ((right_s, right_r), (left_s, left_r))[direction]
+        return copy_to(
+            src.at[k],
+            dst.at[k],
+            gr_s.at[direction, k],
+            gr_r.at[direction, k],
+            me,
+            at_dom(1 - 2 * direction),
+        )
+
+    def to_columns(k):
         at = pl.ds(at_dom(k) * per_chunk, per_chunk)
         rhs = jnp.concatenate(
             [view[at].reshape(chunk, TILE), view2[at].reshape(chunk, TILE)], axis=1
         )
         part = lax.dot_general(own_slope, rhs, NT, preferred_element_type=F32)
-        part = part.astype(BF16).reshape(nz, nx, ROWS, chunk)
+        part = part.reshape(nz, nx, ROWS, chunk)
         for x in range(nx):
-            send_x[k, x] = part[:, x]
+            send_x[k, x] = part[:zx, x].astype(BF16)
         for aside in range(1, nx):
             partial_x(k, aside).start()
+        rest = part[zx:].reshape(ring_rows, chunk)
+        if k == right:
+            right_s[0] = rest.astype(BF16)
+            ring_copy(0, 0).start()
+        elif k == right + 1:
+            left_s[0] = rest.astype(BF16)
+            ring_copy(1, 0).start()
+        else:
+            rest_of[k] = rest
+
+    near_far = [right, right + 1]
+    for k in range(1, right):
+        near_far.append(right - k)
+        if right + 1 + k < ny:
+            near_far.append(right + 1 + k)
+    near_far.append(0)
+    for k in near_far:
+        to_columns(k)
+
+    def ring_step(k):
+        if k < right:
+            wait_bytes(right_r.at[k - 1], gr_r.at[0, k - 1])
+            right_s[k] = (rest_of[right - k] + right_r[k - 1].astype(F32)).astype(BF16)
+            ring_copy(0, k).start()
+        if k < left:
+            wait_bytes(left_r.at[k - 1], gr_r.at[1, k - 1])
+            left_s[k] = (
+                rest_of[right + 1 + k] + left_r[k - 1].astype(F32)
+            ).astype(BF16)
+            ring_copy(1, k).start()
 
     def spread_out(k):
         to = at_dom(k)
@@ -433,21 +494,24 @@
         for aside in range(1, nx):
             total += land_x[k, aside - 1].astype(F32)
         send_z[k] = total.astype(BF16)
-        for step in range(nz):
-            if k == 0 and step == 0:
-                continue
-            z = at_row(step)
-            copy_to(
+        for z in range(zx):
+            tile = copy_to(
                 send_z.at[k, z],
                 land_z.at[row * ny + dom],
                 phase_s.at[5],
                 phase_r.at[5],
                 device(z, col, core),
                 to,
-            ).start()
-
-    for k in range(ny // 2):
+            )
+            if k:
+                tile.start()
+            else:
+                pl.when(row != z)(tile.start)
+
+    for k in near_far[:2]:
         spread_out(k)
+    for k in range(1, right - 1):
+        ring_step(k)
 
     wait_bytes(cols.at[pl.ds(0, nf - 1)], phase_r.at[4])
     shuf[...] = cols[...].reshape(nb * ROWS, TILE).astype(F32)
@@ -477,13 +541,46 @@
         ).start()
     land_d[dom] = send_d[dom]
 
-    for k in range(ny // 2, ny):
+    for k in near_far[2:]:
         spread_out(k)
-    land_z[row * ny + dom] = send_z[0, row]
+    if right > 1:
+        ring_step(right - 1)
+
+    @pl.when(row < zx)
+    def _():
+        land_z[row * ny + dom] = send_z[0, jnp.minimum(row, zx - 1)]
 
     for g in range(GROUPS):
         both = dot(atn_bf[...], back[g])
         own[g] = both[:nb] + both[nb:]
+
+    wait_bytes(right_r.at[right - 1], gr_r.at[0, right - 1])
+    wait_bytes(left_r.at[left - 1], gr_r.at[1, left - 1])
+    send_w[...] = (
+        (
+            rest_of[0]
+            + right_r[right - 1].astype(F32)
+            + left_r[left - 1].astype(F32)
+        )
+        .astype(BF16)
+        .reshape(ring_tiles, ROWS, chunk)
+    )
+    chip = row * nx + col
+    for t in range(ring_tiles):
+        z, x = zx + t // nx, t % nx
+        tile = copy_to(
+            send_w.at[t],
+            land_w.at[chip],
+            phase_s.at[8],
+            phase_r.at[8],
+            device(z, x, core),
+            dom,
+        )
+        pl.when(chip != z * nx + x)(tile.start)
+
+    @pl.when(row >= zx)
+    def _():
+        land_w[chip] = send_w[jnp.maximum(chip - zx * nx, 0)]
 
     wait_bytes(land_d.at[pl.ds(0, ny - 1)], phase_r.at[6])
     landed = land_d[...].reshape(far, width)
@@ -501,11 +598,22 @@
     fg_out = pltpu.make_async_copy(fg_ref, fg_hbm, in_sem.at[10])
     fg_out.start()
 
-    wait_bytes(land_z.at[pl.ds(0, nz * ny - 1)], phase_r.at[5])
-    rows_sum = land_z[0].astype(F32)
-    for m in range(1, nz * ny):
-        rows_sum += land_z[m].astype(F32)
-    send_y[...] = rows_sum * scale
+    @pl.when(row < zx)
+    def _():
+        wait_bytes(land_z.at[pl.ds(0, nz * ny - 1)], phase_r.at[5])
+        rows_sum = land_z[0].astype(F32)
+        for m in range(1, nz * ny):
+            rows_sum += land_z[m].astype(F32)
+        send_y[...] = rows_sum * scale
+
+    @pl.when(row >= zx)
+    def _():
+        wait_bytes(land_w.at[pl.ds(0, chips - 1)], phase_r.at[8])
+        rows_sum = land_w[0].astype(F32)
+        for m in range(1, chips):
+            rows_sum += land_w[m].astype(F32)
+        send_y[...] = rows_sum * scale
+
     for step in range(1, ny):
         to = at_dom(step)
         copy_to(send_y, land_y.at[dom], phase_s.at[7], phase_r.at[7], me, to).start()
@@ -516,7 +624,20 @@
     view_copy.wait_send()
     slope_copy.wait_send()
     wait_bytes(send_g.at[pl.ds(0, nf - 1)], phase_s.at[4])
-    wait_bytes(land_z.at[pl.ds(0, nz * ny - 1)], phase_s.at[5])
+    @pl.when(row < zx)
+    def _():
+        wait_bytes(land_z.at[pl.ds(0, zx * ny - 1)], phase_s.at[5])
+        wait_bytes(land_w.at[pl.ds(0, ring_tiles)], phase_s.at[8])
+
+    @pl.when(row >= zx)
+    def _():
+        wait_bytes(land_z.at[pl.ds(0, zx * ny)], phase_s.at[5])
+        wait_bytes(land_w.at[pl.ds(0, ring_tiles - 1)], phase_s.at[8])
+
+    for k in range(right):
+        ring_copy(0, k).wait_send()
+    for k in range(left):
+        ring_copy(1, k).wait_send()
     wait_bytes(send_d.at[pl.ds(0, ny - 1)], phase_s.at[6])
     for step in order:
         if step:
@@ -535,6 +656,26 @@
     fg_out.wait()
     wg_out.wait()
     wait_bytes(land_y.at[pl.ds(0, ny - 1)], phase_s.at[7])
+
+
+def hand_over(*refs):
+    n = len(refs) // 3
+    ins, outs, held, sem = refs[:n], refs[n : 2 * n], refs[2 * n : 3 * n], refs[-1]
+    fetches = [
+        pltpu.make_async_copy(src, dst, sem.at[0, i])
+        for i, (src, dst) in enumerate(zip(ins, held))
+    ]
+    stores = [
+        pltpu.make_async_copy(src, dst, sem.at[1, i])
+        for i, (src, dst) in enumerate(zip(held, outs))
+    ]
+    for fetch in fetches:
+        fetch.start()
+    for fetch, store in zip(fetches, stores):
+        fetch.wait()
+        store.start()
+    for store in stores:
+        store.wait()
 
 
 def per_device(
@@ -560,6 +701,9 @@
     far = ny * ROWS
     lanes = NBANK * nb
     width = ROWS // GROUPS * TILE
+    ring_rows = (nz - ZX) * nx * ROWS
+    right = ny // 2
+    left = ny - 1 - right
     scale = 1.0 / math.sqrt(ny * features.shape[2])
     hbm = pl.BlockSpec(memory_space=pl.ANY)
     dma = pltpu.SemaphoreType.DMA
@@ -609,16 +753,23 @@
             pltpu.VMEM((GROUPS, nb, width), F32),
             pltpu.VMEM((ny, ROWS, width), BF16),
             pltpu.VMEM((ny, ROWS, width), BF16),
-            pltpu.VMEM((ny, nx, nz, ROWS, chunk), BF16),
-            pltpu.VMEM((ny, nx - 1, nz, ROWS, chunk), BF16),
-            pltpu.VMEM((ny, nz, ROWS, chunk), BF16),
+            pltpu.VMEM((ny, nx, ZX, ROWS, chunk), BF16),
+            pltpu.VMEM((ny, nx - 1, ZX, ROWS, chunk), BF16),
+            pltpu.VMEM((ny, ZX, ROWS, chunk), BF16),
             pltpu.VMEM((nz * ny, ROWS, chunk), BF16),
+            pltpu.VMEM((ny, ring_rows, chunk), F32),
+            pltpu.VMEM((right, ring_rows, chunk), BF16),
+            pltpu.VMEM((right, ring_rows, chunk), BF16),
+            pltpu.VMEM((left, ring_rows, chunk), BF16),
+            pltpu.VMEM((left, ring_rows, chunk), BF16),
+            pltpu.VMEM(((nz - ZX) * nx, ROWS, chunk), BF16),
+            pltpu.VMEM((chips, ROWS, chunk), BF16),
             pltpu.VMEM((ROWS, chunk), F32),
             pltpu.VMEM((ny, ROWS, chunk), F32),
             dma((12,)),
             pltpu.SemaphoreType.REGULAR,
-            dma((8,)),
-            dma((8,)),
+            dma((9,)),
+            dma((9,)),
             dma((nz,)),
             dma((nz,)),
             dma((nz,)),
@@ -627,6 +778,8 @@
             dma((nz,)),
             dma((ny,)),
             dma((ny,)),
+            dma((2, right)),
+            dma((2, right)),
         ],
         compiler_params=pltpu.CompilerParams(
             collective_id=0,
@@ -644,6 +797,16 @@
         counts,
         cotangent[0].reshape(chips, 2, ROWS, TILE),
     )
+    results = (act, feature_grad, weight_grad)
+    act, feature_grad, weight_grad = pl.pallas_call(
+        hand_over,
+        out_shape=tuple(jax.ShapeDtypeStruct(a.shape, a.dtype) for a in results),
+        in_specs=[hbm] * 3,
+        out_specs=(hbm, hbm, hbm),
+        scratch_shapes=[pltpu.VMEM(a.shape, a.dtype) for a in results]
+        + [dma((2, 3))],
+        compiler_params=pltpu.CompilerParams(vmem_limit_bytes=60 * 2**20),
+    )(*results)
     return (
         act.reshape(cotangent.shape),
         feature_grad[None],

time: 70.6 us -> 65.4 us (0.926)
  local copies, waits for them, and re-layouts: 3.21 us -> 0 us
  Pallas kernels: 66.5 us -> 63.9 us
    pallas_call x1, Pallas kernels: 66.5 us -> 62.1 us  [per_device(): pl.pallas_call(functools.partial(kernel, nf, ny, per_pair, scale), out_sh...]
    unnamed x7 -> x0, local copies, waits for them, and re-layouts: 3.21 us -> none
    pallas_call x0 -> x1, Pallas kernels: none -> 1.8 us  [per_device(): pl.pallas_call(hand_over, out_shape=tuple((jax.ShapeDtypeStruct(a.shape,...]
where the time goes in v3:
time: 65.4 us; the launch traced here: 64.6 us
  Pallas kernels  63.9 us (98%)
    pallas_call x1, Pallas kernels, per_device(): pl.pallas_call(functools.partial(kernel, nf, ny, per_pair, scale), out_sh...  62.1 us
    pallas_call x1, Pallas kernels, per_device(): pl.pallas_call(hand_over, out_shape=tuple((jax.ShapeDtypeStruct(a.shape,...  1.8 us

profile of v3, /device:TPU:6, one launch (start us, length us, event | category | flops | bytes accessed | tf_op | source)
XLA Modules:
  0.0 64.6 jit_solution(10786737794982125379)
XLA Ops:
  0.6 62.1 %shard_map.112 = (bf16[32,2,16,128]{3,2,1,0:T(8,128)(2,1)}, bf16[16,8192]{1,0:T(8,128)(2,1)}, f32[16,1024]{1,0:T(8,128)}) custom-call(s32[4,8]{1,0:T(4,128)} %bitcast.20, bf16[16,8192]{1,0:T(8,128)(2,1)} %bitcast.16, bf16[16,1024]{1,0:T(8,128)(2,1)} %w_hbm.1, bf16[4,128,128]{2,1,0:T(8,128)(2,1)} %bank_hbm.1, s32[8,64]{1,0:T(8,128)} %bitcast.18, ...), custom_call_target="tpu_custom_call" | custom-call | tf_op jit(solution)/shard_map/pallas_call | solution.py:710
  62.8 1.8 %shard_map.113 = (bf16[32,2,16,128]{3,2,1,0:T(8,128)(2,1)}, bf16[16,8192]{1,0:T(8,128)(2,1)}, f32[16,1024]{1,0:T(8,128)}) custom-call(bf16[32,2,16,128]{3,2,1,0:T(8,128)(2,1)} %get-tuple-element.9.refs_0_, bf16[16,8192]{1,0:T(8,128)(2,1)} %get-tuple-element.10.refs_1_, f32[16,1024]{1,0:T(8,128)} %get-tuple-element.11.refs_2_), custom_call_target="tpu_custom_call" | custom-call | tf_op jit(solution)/shard_map/pallas_call | solution.py:801

commit v4 on v3

--- a/solution.py
+++ b/solution.py
@@ -508,10 +508,12 @@
             else:
                 pl.when(row != z)(tile.start)
 
-    for k in near_far[:2]:
+    ring_step(1)
+    for k in near_far[:3]:
         spread_out(k)
-    for k in range(1, right - 1):
-        ring_step(k)
+    ring_step(2)
+    for k in near_far[3:]:
+        spread_out(k)
 
     wait_bytes(cols.at[pl.ds(0, nf - 1)], phase_r.at[4])
     shuf[...] = cols[...].reshape(nb * ROWS, TILE).astype(F32)
@@ -541,8 +543,6 @@
         ).start()
     land_d[dom] = send_d[dom]
 
-    for k in near_far[2:]:
-        spread_out(k)
     if right > 1:
         ring_step(right - 1)
 

time: 65.4 us -> 63.5 us (0.971)
  Pallas kernels: 63.9 us -> 62.5 us
    pallas_call x1, Pallas kernels: 62.1 us -> 60.6 us  [per_device(): pl.pallas_call(functools.partial(kernel, nf, ny, per_pair, scale), out_sh...]
where the time goes in v4:
time: 63.5 us; the launch traced here: 63.1 us
  Pallas kernels  62.5 us (98%)
  between operations  0.64 us (1%)
    pallas_call x1, Pallas kernels, per_device(): pl.pallas_call(functools.partial(kernel, nf, ny, per_pair, scale), out_sh...  60.6 us
    pallas_call x1, Pallas kernels, per_device(): pl.pallas_call(hand_over, out_shape=tuple((jax.ShapeDtypeStruct(a.shape,...  1.8 us

profile of v4, /device:TPU:6, one launch (start us, length us, event | category | flops | bytes accessed | tf_op | source)
XLA Modules:
  0.0 63.1 jit_solution(16640084601999922235)
XLA Ops:
  0.6 60.6 %shard_map.112 = (bf16[32,2,16,128]{3,2,1,0:T(8,128)(2,1)}, bf16[16,8192]{1,0:T(8,128)(2,1)}, f32[16,1024]{1,0:T(8,128)}) custom-call(s32[4,8]{1,0:T(4,128)} %bitcast.20, bf16[16,8192]{1,0:T(8,128)(2,1)} %bitcast.16, bf16[16,1024]{1,0:T(8,128)(2,1)} %w_hbm.1, bf16[4,128,128]{2,1,0:T(8,128)(2,1)} %bank_hbm.1, s32[8,64]{1,0:T(8,128)} %bitcast.18, ...), custom_call_target="tpu_custom_call" | custom-call | tf_op jit(solution)/shard_map/pallas_call | solution.py:710
  61.3 1.8 %shard_map.113 = (bf16[32,2,16,128]{3,2,1,0:T(8,128)(2,1)}, bf16[16,8192]{1,0:T(8,128)(2,1)}, f32[16,1024]{1,0:T(8,128)}) custom-call(bf16[32,2,16,128]{3,2,1,0:T(8,128)(2,1)} %get-tuple-element.9.refs_0_, bf16[16,8192]{1,0:T(8,128)(2,1)} %get-tuple-element.10.refs_1_, f32[16,1024]{1,0:T(8,128)} %get-tuple-element.11.refs_2_), custom_call_target="tpu_custom_call" | custom-call | tf_op jit(solution)/shard_map/pallas_call | solution.py:801

commit v5 on v4

--- a/solution.py
+++ b/solution.py
@@ -17,7 +17,7 @@
 F32 = jnp.float32
 BF16 = jnp.bfloat16
 NX = 4
-EARLY = 3
+EARLY = 5
 MIDDLE = 5
 ZX = 4
 

time: 63.5 us -> 63 us (level)
  no operation moved by 1% of the time
where the time goes in v5:
time: 63 us; the launch traced here: 62.8 us
  Pallas kernels  62.2 us (99%)
  between operations  0.64 us (1%)
    pallas_call x1, Pallas kernels, per_device(): pl.pallas_call(functools.partial(kernel, nf, ny, per_pair, scale), out_sh...  60.4 us
    pallas_call x1, Pallas kernels, per_device(): pl.pallas_call(hand_over, out_shape=tuple((jax.ShapeDtypeStruct(a.shape,...  1.8 us

profile of v5, /device:TPU:6, one launch (start us, length us, event | category | flops | bytes accessed | tf_op | source)
XLA Modules:
  0.0 62.8 jit_solution(14241356484964633324)
XLA Ops:
  0.6 60.4 %shard_map.112 = (bf16[32,2,16,128]{3,2,1,0:T(8,128)(2,1)}, bf16[16,8192]{1,0:T(8,128)(2,1)}, f32[16,1024]{1,0:T(8,128)}) custom-call(s32[4,8]{1,0:T(4,128)} %bitcast.20, bf16[16,8192]{1,0:T(8,128)(2,1)} %bitcast.16, bf16[16,1024]{1,0:T(8,128)(2,1)} %w_hbm.1, bf16[4,128,128]{2,1,0:T(8,128)(2,1)} %bank_hbm.1, s32[8,64]{1,0:T(8,128)} %bitcast.18, ...), custom_call_target="tpu_custom_call" | custom-call | tf_op jit(solution)/shard_map/pallas_call | solution.py:710
  61.0 1.8 %shard_map.113 = (bf16[32,2,16,128]{3,2,1,0:T(8,128)(2,1)}, bf16[16,8192]{1,0:T(8,128)(2,1)}, f32[16,1024]{1,0:T(8,128)}) custom-call(bf16[32,2,16,128]{3,2,1,0:T(8,128)(2,1)} %get-tuple-element.9.refs_0_, bf16[16,8192]{1,0:T(8,128)(2,1)} %get-tuple-element.10.refs_1_, f32[16,1024]{1,0:T(8,128)} %get-tuple-element.11.refs_2_), custom_call_target="tpu_custom_call" | custom-call | tf_op jit(solution)/shard_map/pallas_call | solution.py:801
